TPU v7x, 32 devices: a whole 2x2x4 slice. The times are simulated.
32 devices in a mesh: groups: 2 (over y), leaf: 4 (over z), cols: 2 (over x), sub: 2 (over core).
Axes of the slice: x: 2, y: 2, z: 4, core: 2. Of those that a mesh axis runs over, the one named last changes fastest.
Arguments:
- points: bfloat16 [128, 131072], P(('groups', 'cols'), ('leaf', 'sub')), parts along dimension 0, may hold values from -6 to 6
- leaf_basis: bfloat16 [512, 64, 256], P(('leaf', 'sub')), may hold values from -0.375 to 0.375
- transfer: bfloat16 [512, 64, 64], P(('leaf', 'sub')), may hold values from -0.5 to 0.5
- far_list: int32 [512, 8], P(('leaf', 'sub')), may hold values from -1 to 511, as said below
- far_coupling: bfloat16 [512, 64, 512], P(('leaf', 'sub')), may hold values from -0.25 to 0.25
- near_list: int32 [512, 5], P(('leaf', 'sub')), may hold values from -1 to 511, as said below
- near_blocks: bfloat16 [512, 5, 256, 256], P(('leaf', 'sub')), may hold values from -0.15625 to 0.15625
- top_coupling: bfloat16 [8, 64, 512], P(('leaf', 'sub')), may hold values from -0.1875 to 0.1875
Outputs:
- product: bfloat16 [128, 131072], P(('groups', 'cols'), ('leaf', 'sub')), parts along dimension 0
There are 2 independent parts, one for each index of `groups`. A program takes and returns all parts, laid end to end along the dimension named above; an argument that names none is the same for every part. Nothing has to cross between parts.
Inputs may be any that keep to these rules, and one draw needn't show every extreme that they name: `near_list`: each row lists near-field boxes of that leaf box, -1 marking an empty slot; slot 0 holds the box itself, every listed box lies at most 4 boxes away, and no box is listed twice in a row. `far_list`: each row lists far-field partners of that leaf box, -1 marking an empty slot; every listed box lies more than 4 and at most 8 boxes away, and no box is listed twice in a row.
All inputs are finite; a program needn't handle non-finite values.
Results may differ from a plain program's by a relative error of at most 0.0057.
Values may be sent and summed in bfloat16 or wider, within the bound.
No kernel may reach another device: no remote copies, remote signals or barrier semaphores. Data moves between devices by JAX's collectives and lax.ppermute only.
A program may use at most 192 MiB of HBM per device.

v0:
```python
import functools

import jax
import jax.numpy as jnp
from jax import lax
from jax.experimental import pallas as pl
from jax.experimental.pallas import tpu as pltpu
from jax.sharding import PartitionSpec as P

REACH = 4
FREACH = 8
SUBTREE = ("leaf", "sub")
F32 = jnp.float32
BF16 = jnp.bfloat16
LANES = 128
CHUNK = 8
AHEAD = 2
UP_VMEM = 3
UP_COST = 2 * 10**10
MOVING = 3


def dot(a, b, a_dim, b_dim):
    return lax.dot_general(a, b, (((a_dim,), (b_dim,)), ((), ())), preferred_element_type=F32)


def low_half(shape):
    return lax.broadcasted_iota(jnp.int32, shape, len(shape) - 1) < LANES // 2


def point_slice(box, leaf):
    return pl.ds(pl.multiple_of(box * leaf, leaf), leaf)


def spread_pair(joined):
    low = low_half(joined.shape)
    turned = pltpu.roll(joined, LANES // 2, 1)
    return jnp.where(low, joined, turned).astype(BF16), jnp.where(low, turned, joined).astype(BF16)


def near_box(blocks, held, near_list, box, base, empty, leaf):
    moving = None
    fixed = None
    for slot in range(blocks.shape[0]):
        listed = near_list[slot, box]
        place = jnp.where(listed < 0, empty, listed - base)
        source = held[:, point_slice(place, leaf)]
        if slot < MOVING:
            term = dot(source, blocks[slot], 1, 1)
            moving = term if moving is None else moving + term
        else:
            term = dot(blocks[slot], source, 1, 1)
            fixed = term if fixed is None else fixed + term
    return moving + fixed.T


def up_kernel(place_ref, points, basis, transfer, pts, bas, tra, coeffs, inner, outer, flat, sem):
    boxes, rank, leaf = basis.shape
    columns = points.shape[0]
    device = place_ref[0]
    parts = sem.shape[0] - 1
    per = boxes // parts
    copies = []
    for part in range(parts):
        lanes = pl.ds(part * per * leaf, per * leaf)
        here = pl.ds(part * per, per)
        copies.append(
            (
                pltpu.make_async_copy(points.at[:, lanes], pts.at[:, lanes], sem.at[part, 0]),
                pltpu.make_async_copy(basis.at[here], bas.at[here], sem.at[part, 1]),
            )
        )
    whole = pltpu.make_async_copy(transfer, tra, sem.at[parts, 0])
    for a, b in copies:
        a.start()
        b.start()
    whole.start()
    pts[:, boxes * leaf :] = jnp.zeros((columns, leaf), BF16)
    coeffs[boxes] = jnp.zeros((columns, LANES), BF16)
    low = low_half((columns, LANES))
    for part in range(parts):
        for c in copies[part]:
            c.wait()
        for box in range(part * per, (part + 1) * per, 2):
            both = jnp.concatenate(
                [pts[:, box * leaf : (box + 1) * leaf], pts[:, (box + 1) * leaf : (box + 2) * leaf]], 0
            )
            grown = dot(both, bas[box : box + 2].reshape(2 * rank, leaf), 1, 1)
            joined = jnp.where(low, grown[:columns], grown[columns:])
            flat[:, box * rank : (box + 2) * rank] = joined.astype(BF16)
            coeffs[box], coeffs[box + 1] = spread_pair(joined)
    whole.wait()
    root = dot(flat[...], tra[...].reshape(boxes * rank, rank), 1, 0)
    root = jnp.concatenate([root, root], 1).astype(BF16)
    near_blocks = REACH * leaf // LANES
    far_blocks = FREACH * rank // LANES
    odd = lax.rem(device, 2)
    for pay, at_start in ((inner, odd), (outer, 1 - odd)):
        first = jnp.where(at_start == 1, 0, (boxes - REACH) * leaf)
        for i in range(near_blocks):
            pay[i] = pts[:, pl.ds(pl.multiple_of(first + i * LANES, LANES), LANES)]
        first = jnp.where(at_start == 1, 0, (boxes - FREACH) * rank)
        for i in range(far_blocks):
            pay[near_blocks + i] = flat[:, pl.ds(pl.multiple_of(first + i * LANES, LANES), LANES)]
    inner[near_blocks + far_blocks] = root


def down_kernel(order, place_ref, near_list, far_list, *refs):
    pts, coeffs, basis, transfer, coupling, top, blocks, roots, inner, outer, out = refs[:11]
    edge_pts, edge_coeffs, stage, sem, out_sem = refs[11:]
    boxes, slots, leaf = blocks.shape[:3]
    rank = basis.shape[1]
    columns = pts.shape[0]
    far_slots = far_list.shape[0]
    device = place_ref[0]
    base = device * boxes
    near_blocks = REACH * leaf // LANES
    far_blocks = FREACH * rank // LANES
    chunks = boxes // CHUNK

    def in_copy(c):
        here = pl.ds(c * CHUNK, CHUNK)
        return pltpu.make_async_copy(coupling.at[here], cou.at[here], sem.at[c])

    def out_copy(c):
        lanes = pl.ds(c * CHUNK * leaf, CHUNK * leaf)
        return pltpu.make_async_copy(stage.at[:, lanes], out.at[:, lanes], out_sem.at[c])


    low = low_half((columns, LANES))
    lane = lax.broadcasted_iota(jnp.int32, (columns, LANES), 1)
    total = jnp.zeros((columns, rank), F32)
    for i in range(0, len(order), 2):
        owner = jnp.bitwise_xor(device, order[i])
        odd = lax.rem(owner, 2)
        even_owner = owner - odd
        both = jnp.where(lane // (LANES // 2) == odd, roots[i], roots[i + 1])
        owners = even_owner + lane // (LANES // 2)
        both = jnp.where(jnp.abs(owners - device) >= 2, both, jnp.zeros((), BF16))
        weights = top[0, :, pl.ds(pl.multiple_of(even_owner * rank, 2 * rank), 2 * rank)]
        total = total + dot(both, weights, 1, 1)
    high_part = total.astype(BF16)
    rest = (total - high_part.astype(F32)).astype(BF16)
    top_parts = jnp.concatenate([high_part, rest], 0)

    near_span = CHUNK + 2 * REACH
    far_span = CHUNK + 2 * FREACH
    near_first = (-REACH, boxes - CHUNK - REACH)
    far_first = (-FREACH, boxes - CHUNK - FREACH)
    for edge in range(2):
        skip = (1 - edge) * REACH
        first = near_first[edge] + skip
        edge_pts[edge, :, skip * leaf : (skip + CHUNK + REACH) * leaf] = pts[
            :, first * leaf : (first + CHUNK + REACH) * leaf
        ]
        edge_pts[edge, :, near_span * leaf :] = jnp.zeros((columns, leaf), BF16)
        skip = (1 - edge) * FREACH
        first = far_first[edge] + skip
        edge_coeffs[edge, skip : skip + CHUNK + FREACH] = coeffs[first : first + CHUNK + FREACH]
        edge_coeffs[edge, far_span] = jnp.zeros((columns, LANES), BF16)

    def halo(edge, source):
        first = edge * (CHUNK + REACH) * leaf
        for i in range(near_blocks):
            edge_pts[edge, :, first + i * LANES : first + (i + 1) * LANES] = source[i]
        first = edge * (CHUNK + FREACH)
        for i in range(far_blocks):
            even, odd = spread_pair(source[near_blocks + i].astype(F32))
            edge_coeffs[edge, first + 2 * i] = even
            edge_coeffs[edge, first + 2 * i + 1] = odd

    @pl.when(lax.rem(device, 2) == 0)
    def _():
        halo(0, outer)
        halo(1, inner)

    @pl.when(lax.rem(device, 2) == 1)
    def _():
        halo(0, inner)
        halo(1, outer)

    row = lax.broadcasted_iota(jnp.int32, (2 * columns, LANES), 0)
    lane2 = lax.broadcasted_iota(jnp.int32, (2 * columns, LANES), 1)
    own_half = row // columns == lane2 // (LANES // 2)

    for c in range(chunks):
        if c == 0 or c == chunks - 1:
            edge = 0 if c == 0 else 1
            near_held, near_base, near_empty = edge_pts.at[edge], base + near_first[edge], near_span
            far_held, far_base, far_empty = edge_coeffs.at[edge], base + far_first[edge], far_span
        else:
            near_held, near_base, near_empty = pts, base, boxes
            far_held, far_base, far_empty = coeffs, base, boxes
        first = c * CHUNK
        down = dot(top_parts, transfer[first : first + CHUNK].reshape(CHUNK * rank, rank), 1, 1)
        down = down[:columns] + down[columns:]
        fars = []
        for pair in range(CHUNK // 2):
            rows = []
            for side in range(2):
                box = first + 2 * pair + side
                pieces = []
                for slot in range(0, far_slots, 2):
                    taken = []
                    for s in range(2):
                        listed = far_list[slot + s, box]
                        taken.append(far_held[jnp.where(listed < 0, far_empty, listed - far_base)])
                    pieces.append(jnp.where(low, taken[0], taken[1]))
                rows.append(jnp.concatenate(pieces, 1))
            box = first + 2 * pair
            weights = coupling[box : box + 2].reshape(2 * rank, far_slots * rank)
            fars.append(dot(jnp.concatenate(rows, 0), weights, 1, 1))
        nears = [
            near_box(blocks.at[first + i], near_held, near_list, first + i, near_base, near_empty, leaf)
            for i in range(CHUNK)
        ]
        for pair in range(CHUNK // 2):
            box = first + 2 * pair
            far = jnp.where(low, fars[pair][:columns], fars[pair][columns:])
            far = (far + down[:, pair * LANES : (pair + 1) * LANES]).astype(BF16)
            spread = jnp.where(own_half, jnp.concatenate([far, far], 0), jnp.zeros((), BF16))
            spread = dot(spread, basis[box : box + 2].reshape(2 * rank, leaf), 1, 0)
            for side in range(2):
                stage[:, (box + side) * leaf : (box + side + 1) * leaf] = (
                    spread[side * columns : (side + 1) * columns] + nears[2 * pair + side]
                ).astype(BF16)
        out_copy(c).start()
    for c in range(chunks):
        out_copy(c).wait()


def in_vmem(x):
    return pltpu.with_memory_space_constraint(x, pltpu.VMEM)


def in_hbm(x):
    return pltpu.with_memory_space_constraint(x, pltpu.HBM)


def shards(
    points, leaf_basis, transfer, far_list, far_coupling, near_list, near_blocks, top_coupling
):
    columns = points.shape[0]
    boxes, rank, leaf = leaf_basis.shape
    size = lax.axis_size("leaf") * lax.axis_size("sub")
    rounds = size.bit_length() - 1
    device = lax.axis_index(SUBTREE)
    place = device[None].astype(jnp.int32)
    hbm = pl.BlockSpec(memory_space=pl.ANY)
    vmem = pl.BlockSpec(memory_space=pltpu.VMEM)
    smem = pl.BlockSpec(memory_space=pltpu.SMEM)
    halo = REACH * leaf // LANES + FREACH * rank // LANES

    parts = 4
    pts, bas, tra, coeffs, inner, outer = pl.pallas_call(
        up_kernel,
        out_shape=[
            pltpu.VMEM((columns, (boxes + 1) * leaf), BF16),
            pltpu.VMEM((boxes, rank, leaf), BF16),
            pltpu.VMEM((boxes, rank, rank), BF16),
            pltpu.VMEM((boxes + 1, columns, LANES), BF16),
            pltpu.VMEM((halo + 1, columns, LANES), BF16),
            pltpu.VMEM((halo, columns, LANES), BF16),
        ],
        in_specs=[smem, hbm, hbm, hbm],
        out_specs=[vmem] * 6,
        scratch_shapes=[
            pltpu.VMEM((columns, boxes * rank), BF16),
            pltpu.SemaphoreType.DMA((parts + 1, 2)),
        ],
        compiler_params=pltpu.CompilerParams(vmem_limit_bytes=UP_VMEM * 2**20),
        cost_estimate=pl.CostEstimate(flops=UP_COST, bytes_accessed=2 * boxes * rank * leaf, transcendentals=0),
        name="upward",
    )(place, in_hbm(points), in_hbm(leaf_basis), in_hbm(transfer))

    inner_got = lax.ppermute(inner, SUBTREE, [(i, i ^ 1) for i in range(size)])
    outer_pairs = [(i, i + 1) for i in range(1, size - 1, 2)]
    outer_got = lax.ppermute(outer, SUBTREE, outer_pairs + [(j, i) for i, j in outer_pairs])
    roots = jnp.concatenate([inner[halo:], inner_got[halo:]], 0)
    order = [0, 1]
    for step in range(1, rounds):
        if step == rounds - 1:
            roots, outer_got = lax.optimization_barrier((roots, outer_got))
        flip = (2 << step) - 1
        got = lax.ppermute(roots, SUBTREE, [(i, i ^ flip) for i in range(size)])
        roots = jnp.concatenate([roots, got], 0)
        order = order + [flip ^ o for o in order]

    far = far_coupling
    held = [pts, coeffs, bas, tra, far_coupling, top_coupling, near_blocks, roots, inner_got, outer_got]
    placed = [in_vmem(x) for x in held]
    return pl.pallas_call(
        functools.partial(down_kernel, order),
        out_shape=jax.ShapeDtypeStruct((columns, boxes * leaf), BF16),
        in_specs=[smem, smem, smem] + [vmem for x in held],
        out_specs=hbm,
        scratch_shapes=[
            pltpu.VMEM((2, columns, (CHUNK + 2 * REACH + 1) * leaf), BF16),
            pltpu.VMEM((2, CHUNK + 2 * FREACH + 1, columns, LANES), BF16),
            pltpu.VMEM((columns, boxes * leaf), BF16),
            pltpu.SemaphoreType.DMA((boxes // CHUNK,)),
            pltpu.SemaphoreType.DMA((boxes // CHUNK,)),
        ],
        compiler_params=pltpu.CompilerParams(vmem_limit_bytes=4 * 2**20),
        name="downward",
    )(place, near_list.T, far_list.T, *placed)


def solution(mesh):
    in_specs = (
        P(("groups", "cols"), SUBTREE),
        P(SUBTREE, None, None),
        P(SUBTREE, None, None),
        P(SUBTREE, None),
        P(SUBTREE, None, None),
        P(SUBTREE, None),
        P(SUBTREE, None, None, None),
        P(SUBTREE, None, None),
    )
    out_specs = P(("groups", "cols"), SUBTREE)
    return jax.shard_map(shards, mesh=mesh, in_specs=in_specs, out_specs=out_specs, check_vma=False)
```

profile of v0, /device:TPU:1, one launch (start us, length us, event | category | flops | bytes accessed | tf_op | source)
XLA Modules:
  0.0 32.6 jit_solution(4843878780772108491)
XLA Ops:
  0.0 0.0 copy-start
  0.0 0.0 copy-start.1
  0.0 0.0 copy-start.2
  0.0 0.0 copy-start.3
  0.0 0.0 copy-start.4
  0.0 3.3 %upward.1 = (bf16[32,16640]{1,0:T(8,128)(2,1)S(1)}, bf16[64,64,256]{2,1,0:T(8,128)(2,1)S(1)}, bf16[64,64,64]{2,1,0:T(8,128)(2,1)S(1)}, bf16[65,32,128]{2,1,0:T(8...) custom-call(s32[1]{0:T(128)} %bitcast.place_ref, bf16[32,16384]{1,0:T(8,128)(2,1)} %points.1, ...), custom_call_target="tpu_custom_call" | custom-call | flops 20000000000 | bytes 2097152 | tf_op jit(solution)/shard_map/upward/pallas_call | solution.py:255
  3.3 0.1 collective-permute-start
  3.4 1.3 %collective-permute-done.refs_8_ = bf16[13,32,128]{2,1,0:T(8,128)(2,1)S(1)} collective-permute-done((bf16[13,32,128]{2,1,0:T(8,128)(2,1)S(1)}, bf16[13,32,128]{2,1,0:T(8,128)(2,1)S(1)}, u32[]{:S(2)}, u32[]{:S(2)}) %collective-permute-start) | collective-permute-done | bytes 106528 | tf_op jit(solution)/shard_map/ppermute | solution.py:276
  4.7 2.7 %collective-permute-start.1 = (bf16[2,32,128]{2,1,0:T(8,128)(2,1)S(1)}, bf16[2,32,128]{2,1,0:T(8,128)(2,1)S(1)}, u32[]{:S(2)}, u32[]{:S(2)}) collective-permute-start(bf16[2,32,128]{2,1,0:T(8,128)(2,1)S(1)} %pad_maximum_fusion.2), channel_id=1, source_target_pairs={{0,5},{1,4},{4,1},{5,0},{8,13},{9,12},{12,9},{13,8},{2,7},{3,6},{6... | collective-permute-start | bytes 49160 | tf_op jit(solution)/shard_map/ppermute | solution.py:285
  7.4 2.3 %collective-permute-start.2 = (bf16[12,32,128]{2,1,0:T(8,128)(2,1)S(1)}, bf16[12,32,128]{2,1,0:T(8,128)(2,1)S(1)}, u32[]{:S(2)}, u32[]{:S(2)}) collective-permute-start(bf16[12,32,128]{2,1,0:T(8,128)(2,1)S(1)} %get-tuple-element.18), channel_id=1, source_target_pairs={{1,4},{5,8},{9,12},{4,1},{8,5},{12,9},{3,6},{7,10},{11,14},{6,3},{... | collective-permute-start | bytes 294920 | tf_op jit(solution)/shard_map/ppermute | solution.py:278
  9.7 0.0 collective-permute-done.1
  9.7 4.3 %collective-permute-done.2.refs_9_ = bf16[12,32,128]{2,1,0:T(8,128)(2,1)S(1)} collective-permute-done((bf16[12,32,128]{2,1,0:T(8,128)(2,1)S(1)}, bf16[12,32,128]{2,1,0:T(8,128)(2,1)S(1)}, u32[]{:S(2)}, u32[]{:S(2)}) %collective-permute-start.2) | collective-permute-done | bytes 98336 | tf_op jit(solution)/shard_map/ppermute | solution.py:278
  14.0 1.9 %collective-permute-start.3 = (bf16[4,32,128]{2,1,0:T(8,128)(2,1)S(1)}, bf16[4,32,128]{2,1,0:T(8,128)(2,1)S(1)}, u32[]{:S(2)}, u32[]{:S(2)}) collective-permute-start(bf16[4,32,128]{2,1,0:T(8,128)(2,1)S(1)} %pad_maximum_fusion.1), channel_id=1, source_target_pairs={{0,13},{1,12},{4,9},{5,8},{8,5},{9,4},{12,1},{13,0},{2,15},{3,14},... | collective-permute-start | bytes 98312 | tf_op jit(solution)/shard_map/ppermute | solution.py:285
  15.9 3.3 %collective-permute-done.3 = bf16[4,32,128]{2,1,0:T(8,128)(2,1)S(1)} collective-permute-done((bf16[4,32,128]{2,1,0:T(8,128)(2,1)S(1)}, bf16[4,32,128]{2,1,0:T(8,128)(2,1)S(1)}, u32[]{:S(2)}, u32[]{:S(2)}) %collective-permute-start.3) | collective-permute-done | bytes 32800 | tf_op jit(solution)/shard_map/ppermute | solution.py:285
  19.2 0.0 copy-done
  19.2 0.0 copy-done.1
  19.2 0.0 copy-done.2
  19.2 0.0 copy-done.3
  19.2 0.0 copy-done.4
  19.2 13.4 %downward.1 = bf16[32,16384]{1,0:T(8,128)(2,1)} custom-call(s32[1]{0:T(128)} %bitcast.place_ref, s32[5,64]{1,0:T(8,128)S(1)} %bitcast.3, s32[8,64]{1,0:T(8,128)S(1)} %bitcast.4, bf16[32,16640]{1,0:T(8,128)(2,1)S(1)} %get-tuple-element.13.refs_0_, bf16[65,32,128]{2,1,0:T(8,128)(2,1)S(1)} %get-tuple-element.14.refs_1_, ...), custom_call_target="tpu_custom_call" | custom-call | tf_op jit(solution)/shard_map/downward/pallas_call | solution.py:292
  (5 shorter events, 0.0 us)
Async XLA Ops:
  0.0 19.2 %copy-start = (bf16[64,5,256,256]{3,2,1,0:T(8,128)(2,1)S(1)}, bf16[64,5,256,256]{3,2,1,0:T(8,128)(2,1)}, u32[]{:S(2)}) copy-start(bf16[64,5,256,256]{3,2,1,0:T(8,128)(2,1)} %refs_6_.1) | copy-start | bytes 125829120
  0.0 19.2 %copy-start.1 = (bf16[64,64,512]{2,1,0:T(8,128)(2,1)S(1)}, bf16[64,64,512]{2,1,0:T(8,128)(2,1)}, u32[]{:S(2)}) copy-start(bf16[64,64,512]{2,1,0:T(8,128)(2,1)} %refs_4_.1) | copy-start | bytes 12582916
  0.0 19.2 %copy-start.2 = (bf16[1,64,512]{2,1,0:T(8,128)(2,1)S(1)}, bf16[1,64,512]{2,1,0:T(8,128)(2,1)}, u32[]{:S(2)}) copy-start(bf16[1,64,512]{2,1,0:T(8,128)(2,1)} %refs_5_.1) | copy-start | bytes 196612
  0.0 19.2 %copy-start.3 = (s32[64,5]{0,1:T(8,128)S(1)}, s32[64,5]{0,1:T(8,128)}, u32[]{:S(2)}) copy-start(s32[64,5]{0,1:T(8,128)} %param.13) | copy-start | bytes 3844
  0.0 19.2 %copy-start.4 = (s32[64,8]{0,1:T(8,128)S(1)}, s32[64,8]{0,1:T(8,128)}, u32[]{:S(2)}) copy-start(s32[64,8]{0,1:T(8,128)} %param.11) | copy-start | bytes 6148
  3.3 1.4 %collective-permute-start = (bf16[13,32,128]{2,1,0:T(8,128)(2,1)S(1)}, bf16[13,32,128]{2,1,0:T(8,128)(2,1)S(1)}, u32[]{:S(2)}, u32[]{:S(2)}) collective-permute-start(bf16[13,32,128]{2,1,0:T(8,128)(2,1)S(1)} %get-tuple-element.17), channel_id=1, source_target_pairs={{0,1},{1,0},{4,5},{5,4},{8,9},{9,8},{12,13},{13,12},{2,3},{3,2},{6... | collective-permute-start | bytes 319496 | tf_op jit(solution)/shard_map/ppermute | solution.py:276
  4.7 5.0 %collective-permute-start.1 = (bf16[2,32,128]{2,1,0:T(8,128)(2,1)S(1)}, bf16[2,32,128]{2,1,0:T(8,128)(2,1)S(1)}, u32[]{:S(2)}, u32[]{:S(2)}) collective-permute-start(bf16[2,32,128]{2,1,0:T(8,128)(2,1)S(1)} %pad_maximum_fusion.2), channel_id=1, source_target_pairs={{0,5},{1,4},{4,1},{5,0},{8,13},{9,12},{12,9},{13,8},{2,7},{3,6},{6... | collective-permute-start | bytes 49160 | tf_op jit(solution)/shard_map/ppermute | solution.py:285
  7.4 6.7 %collective-permute-start.2 = (bf16[12,32,128]{2,1,0:T(8,128)(2,1)S(1)}, bf16[12,32,128]{2,1,0:T(8,128)(2,1)S(1)}, u32[]{:S(2)}, u32[]{:S(2)}) collective-permute-start(bf16[12,32,128]{2,1,0:T(8,128)(2,1)S(1)} %get-tuple-element.18), channel_id=1, source_target_pairs={{1,4},{5,8},{9,12},{4,1},{8,5},{12,9},{3,6},{7,10},{11,14},{6,3},{... | collective-permute-start | bytes 294920 | tf_op jit(solution)/shard_map/ppermute | solution.py:278
  14.0 5.1 %collective-permute-start.3 = (bf16[4,32,128]{2,1,0:T(8,128)(2,1)S(1)}, bf16[4,32,128]{2,1,0:T(8,128)(2,1)S(1)}, u32[]{:S(2)}, u32[]{:S(2)}) collective-permute-start(bf16[4,32,128]{2,1,0:T(8,128)(2,1)S(1)} %pad_maximum_fusion.1), channel_id=1, source_target_pairs={{0,13},{1,12},{4,9},{5,8},{8,5},{9,4},{12,1},{13,0},{2,15},{3,14},... | collective-permute-start | bytes 98312 | tf_op jit(solution)/shard_map/ppermute | solution.py:285
where the time goes:
time: 32.8 us; the launch traced here: 32.6 us
  Pallas kernels  16.7 us (51%)
  waiting for transfers between devices  8.85 us (27%)
  starting transfers between devices  6.97 us (21%)
    pallas_call x1, Pallas kernels, shards(): pl.pallas_call(functools.partial(down_kernel, order), out_shape=jax.Shape...  13.4 us
    ppermute x2, starting transfers between devices, shards(): got = lax.ppermute(roots, SUBTREE, [(i, i ^ flip) for i in range(size)])  4.55 us
    ppermute x1, waiting for transfers between devices, shards(): lax.ppermute(outer, SUBTREE, outer_pairs + [(j, i) for i, j in outer_pairs])  4.33 us
    pallas_call x1, Pallas kernels, shards(): pl.pallas_call(up_kernel, out_shape=[pltpu.VMEM((columns, (boxes + 1) * l...  3.27 us
    ppermute x2, waiting for transfers between devices, shards(): got = lax.ppermute(roots, SUBTREE, [(i, i ^ flip) for i in range(size)])  3.26 us
    ppermute x1, starting transfers between devices, shards(): lax.ppermute(outer, SUBTREE, outer_pairs + [(j, i) for i, j in outer_pairs])  2.31 us
    ppermute x1, waiting for transfers between devices, shards(): inner_got = lax.ppermute(inner, SUBTREE, [(i, i ^ 1) for i in range(size)])  1.27 us
  transfers between devices with their start and end apart: 4, of which 3 were waited for; matrix products, arithmetic and copies ran while one was open for 0% of the time, Pallas kernels for 0%

commit v1 on v0

--- a/solution.py
+++ b/solution.py
@@ -14,10 +14,9 @@
 BF16 = jnp.bfloat16
 LANES = 128
 CHUNK = 8
-AHEAD = 2
 UP_VMEM = 3
 UP_COST = 2 * 10**10
-MOVING = 3
+MOVING = 2
 
 
 def dot(a, b, a_dim, b_dim):
@@ -107,7 +106,7 @@
 
 def down_kernel(order, place_ref, near_list, far_list, *refs):
     pts, coeffs, basis, transfer, coupling, top, blocks, roots, inner, outer, out = refs[:11]
-    edge_pts, edge_coeffs, stage, sem, out_sem = refs[11:]
+    edge_pts, edge_coeffs, stage, out_sem = refs[11:]
     boxes, slots, leaf = blocks.shape[:3]
     rank = basis.shape[1]
     columns = pts.shape[0]
@@ -117,10 +116,6 @@
     near_blocks = REACH * leaf // LANES
     far_blocks = FREACH * rank // LANES
     chunks = boxes // CHUNK
-
-    def in_copy(c):
-        here = pl.ds(c * CHUNK, CHUNK)
-        return pltpu.make_async_copy(coupling.at[here], cou.at[here], sem.at[c])
 
     def out_copy(c):
         lanes = pl.ds(c * CHUNK * leaf, CHUNK * leaf)
@@ -279,14 +274,11 @@
     roots = jnp.concatenate([inner[halo:], inner_got[halo:]], 0)
     order = [0, 1]
     for step in range(1, rounds):
-        if step == rounds - 1:
-            roots, outer_got = lax.optimization_barrier((roots, outer_got))
-        flip = (2 << step) - 1
+        flip = 1 << step
         got = lax.ppermute(roots, SUBTREE, [(i, i ^ flip) for i in range(size)])
         roots = jnp.concatenate([roots, got], 0)
         order = order + [flip ^ o for o in order]
 
-    far = far_coupling
     held = [pts, coeffs, bas, tra, far_coupling, top_coupling, near_blocks, roots, inner_got, outer_got]
     placed = [in_vmem(x) for x in held]
     return pl.pallas_call(
@@ -298,7 +290,6 @@
             pltpu.VMEM((2, columns, (CHUNK + 2 * REACH + 1) * leaf), BF16),
             pltpu.VMEM((2, CHUNK + 2 * FREACH + 1, columns, LANES), BF16),
             pltpu.VMEM((columns, boxes * leaf), BF16),
-            pltpu.SemaphoreType.DMA((boxes // CHUNK,)),
             pltpu.SemaphoreType.DMA((boxes // CHUNK,)),
         ],
         compiler_params=pltpu.CompilerParams(vmem_limit_bytes=4 * 2**20),

time: 32.8 us -> 31.3 us (0.954)
  waiting for transfers between devices: 8.85 us -> 4.78 us
  starting transfers between devices: 6.97 us -> 10.1 us
  Pallas kernels: 16.7 us -> 16.1 us
    ppermute x1, starting transfers between devices: 2.31 us -> 5.13 us  [shards(): lax.ppermute(outer, SUBTREE, outer_pairs + [(j, i) for i, j in outer_pairs])]
    ppermute x2, waiting for transfers between devices: 3.26 us -> 1.13 us  [shards(): got = lax.ppermute(roots, SUBTREE, [(i, i ^ flip) for i in range(size)])]
    ppermute x1, waiting for transfers between devices: 4.33 us -> 2.39 us  [shards(): lax.ppermute(outer, SUBTREE, outer_pairs + [(j, i) for i, j in outer_pairs])]
    pallas_call x1, Pallas kernels: 13.4 us -> 12.8 us  [shards(): pl.pallas_call(functools.partial(down_kernel, order), out_shape=jax.Shape...]
    ppermute x2, starting transfers between devices: 4.55 us -> 4.9 us  [shards(): got = lax.ppermute(roots, SUBTREE, [(i, i ^ flip) for i in range(size)])]
where the time goes in v1:
time: 31.3 us; the launch traced here: 31.1 us
  Pallas kernels  16.1 us (51%)
  starting transfers between devices  10.1 us (32%)
  waiting for transfers between devices  4.78 us (15%)
    pallas_call x1, Pallas kernels, shards(): pl.pallas_call(functools.partial(down_kernel, order), out_shape=jax.Shape...  12.8 us
    ppermute x1, starting transfers between devices, shards(): lax.ppermute(outer, SUBTREE, outer_pairs + [(j, i) for i, j in outer_pairs])  5.13 us
    ppermute x2, starting transfers between devices, shards(): got = lax.ppermute(roots, SUBTREE, [(i, i ^ flip) for i in range(size)])  4.9 us
    pallas_call x1, Pallas kernels, shards(): pl.pallas_call(up_kernel, out_shape=[pltpu.VMEM((columns, (boxes + 1) * l...  3.27 us
    ppermute x1, waiting for transfers between devices, shards(): lax.ppermute(outer, SUBTREE, outer_pairs + [(j, i) for i, j in outer_pairs])  2.39 us
    ppermute x1, waiting for transfers between devices, shards(): inner_got = lax.ppermute(inner, SUBTREE, [(i, i ^ 1) for i in range(size)])  1.27 us
    ppermute x2, waiting for transfers between devices, shards(): got = lax.ppermute(roots, SUBTREE, [(i, i ^ flip) for i in range(size)])  1.13 us
  transfers between devices with their start and end apart: 4, of which 3 were waited for; matrix products, arithmetic and copies ran while one was open for 0% of the time, Pallas kernels for 0%

profile of v1, /device:TPU:1, one launch (start us, length us, event | category | flops | bytes accessed | tf_op | source)
XLA Modules:
  0.0 31.1 jit_solution(7069841460543237923)
XLA Ops:
  0.0 0.0 copy-start
  0.0 0.0 copy-start.1
  0.0 0.0 copy-start.2
  0.0 0.0 copy-start.3
  0.0 0.0 copy-start.4
  0.0 3.3 %upward.1 = (bf16[32,16640]{1,0:T(8,128)(2,1)S(1)}, bf16[64,64,256]{2,1,0:T(8,128)(2,1)S(1)}, bf16[64,64,64]{2,1,0:T(8,128)(2,1)S(1)}, bf16[65,32,128]{2,1,0:T(8...) custom-call(s32[1]{0:T(128)} %bitcast.place_ref, bf16[32,16384]{1,0:T(8,128)(2,1)} %points.1, ...), custom_call_target="tpu_custom_call" | custom-call | flops 20000000000 | bytes 2097152 | tf_op jit(solution)/shard_map/upward/pallas_call | solution.py:250
  3.3 0.1 collective-permute-start
  3.4 1.3 %collective-permute-done.refs_8_ = bf16[13,32,128]{2,1,0:T(8,128)(2,1)S(1)} collective-permute-done((bf16[13,32,128]{2,1,0:T(8,128)(2,1)S(1)}, bf16[13,32,128]{2,1,0:T(8,128)(2,1)S(1)}, u32[]{:S(2)}, u32[]{:S(2)}) %collective-permute-start) | collective-permute-done | bytes 106528 | tf_op jit(solution)/shard_map/ppermute | solution.py:271
  4.7 2.4 %collective-permute-start.1 = (bf16[2,32,128]{2,1,0:T(8,128)(2,1)S(1)}, bf16[2,32,128]{2,1,0:T(8,128)(2,1)S(1)}, u32[]{:S(2)}, u32[]{:S(2)}) collective-permute-start(bf16[2,32,128]{2,1,0:T(8,128)(2,1)S(1)} %pad_maximum_fusion.2), channel_id=1, source_target_pairs={{0,4},{1,5},{4,0},{5,1},{8,12},{9,13},{12,8},{13,9},{2,6},{3,7},{6... | collective-permute-start | bytes 49160 | tf_op jit(solution)/shard_map/ppermute | solution.py:278
  7.1 1.1 %collective-permute-done.1 = bf16[2,32,128]{2,1,0:T(8,128)(2,1)S(1)} collective-permute-done((bf16[2,32,128]{2,1,0:T(8,128)(2,1)S(1)}, bf16[2,32,128]{2,1,0:T(8,128)(2,1)S(1)}, u32[]{:S(2)}, u32[]{:S(2)}) %collective-permute-start.1) | collective-permute-done | bytes 16416 | tf_op jit(solution)/shard_map/ppermute | solution.py:278
  8.3 2.5 %collective-permute-start.2 = (bf16[4,32,128]{2,1,0:T(8,128)(2,1)S(1)}, bf16[4,32,128]{2,1,0:T(8,128)(2,1)S(1)}, u32[]{:S(2)}, u32[]{:S(2)}) collective-permute-start(bf16[4,32,128]{2,1,0:T(8,128)(2,1)S(1)} %pad_maximum_fusion.1), channel_id=1, source_target_pairs={{0,8},{1,9},{4,12},{5,13},{8,0},{9,1},{12,4},{13,5},{2,10},{3,11},... | collective-permute-start | bytes 98312 | tf_op jit(solution)/shard_map/ppermute | solution.py:278
  10.7 5.1 %collective-permute-start.3 = (bf16[12,32,128]{2,1,0:T(8,128)(2,1)S(1)}, bf16[12,32,128]{2,1,0:T(8,128)(2,1)S(1)}, u32[]{:S(2)}, u32[]{:S(2)}) collective-permute-start(bf16[12,32,128]{2,1,0:T(8,128)(2,1)S(1)} %get-tuple-element.16), channel_id=1, source_target_pairs={{1,4},{5,8},{9,12},{4,1},{8,5},{12,9},{3,6},{7,10},{11,14},{6,3},{... | collective-permute-start | bytes 294920 | tf_op jit(solution)/shard_map/ppermute | solution.py:273
  15.9 0.0 collective-permute-done.2
  15.9 2.4 %collective-permute-done.3.refs_9_ = bf16[12,32,128]{2,1,0:T(8,128)(2,1)S(1)} collective-permute-done((bf16[12,32,128]{2,1,0:T(8,128)(2,1)S(1)}, bf16[12,32,128]{2,1,0:T(8,128)(2,1)S(1)}, u32[]{:S(2)}, u32[]{:S(2)}) %collective-permute-start.3) | collective-permute-done | bytes 98336 | tf_op jit(solution)/shard_map/ppermute | solution.py:273
  18.3 0.0 copy-done
  18.3 0.0 copy-done.1
  18.3 0.0 copy-done.2
  18.3 0.0 copy-done.3
  18.3 0.0 copy-done.4
  18.3 12.8 %downward.1 = bf16[32,16384]{1,0:T(8,128)(2,1)} custom-call(s32[1]{0:T(128)} %bitcast.place_ref, s32[5,64]{1,0:T(8,128)S(1)} %bitcast.3, s32[8,64]{1,0:T(8,128)S(1)} %bitcast.4, bf16[32,16640]{1,0:T(8,128)(2,1)S(1)} %get-tuple-element.11.refs_0_, bf16[65,32,128]{2,1,0:T(8,128)(2,1)S(1)} %get-tuple-element.12.refs_1_, ...), custom_call_target="tpu_custom_call" | custom-call | tf_op jit(solution)/shard_map/downward/pallas_call | solution.py:284
  (5 shorter events, 0.0 us)
Async XLA Ops:
  0.0 18.3 %copy-start = (bf16[64,5,256,256]{3,2,1,0:T(8,128)(2,1)S(1)}, bf16[64,5,256,256]{3,2,1,0:T(8,128)(2,1)}, u32[]{:S(2)}) copy-start(bf16[64,5,256,256]{3,2,1,0:T(8,128)(2,1)} %refs_6_.1) | copy-start | bytes 125829120
  0.0 18.3 %copy-start.1 = (bf16[64,64,512]{2,1,0:T(8,128)(2,1)S(1)}, bf16[64,64,512]{2,1,0:T(8,128)(2,1)}, u32[]{:S(2)}) copy-start(bf16[64,64,512]{2,1,0:T(8,128)(2,1)} %refs_4_.1) | copy-start | bytes 12582916
  0.0 18.3 %copy-start.2 = (bf16[1,64,512]{2,1,0:T(8,128)(2,1)S(1)}, bf16[1,64,512]{2,1,0:T(8,128)(2,1)}, u32[]{:S(2)}) copy-start(bf16[1,64,512]{2,1,0:T(8,128)(2,1)} %refs_5_.1) | copy-start | bytes 196612
  0.0 18.3 %copy-start.3 = (s32[64,5]{0,1:T(8,128)S(1)}, s32[64,5]{0,1:T(8,128)}, u32[]{:S(2)}) copy-start(s32[64,5]{0,1:T(8,128)} %param.13) | copy-start | bytes 3844
  0.0 18.3 %copy-start.4 = (s32[64,8]{0,1:T(8,128)S(1)}, s32[64,8]{0,1:T(8,128)}, u32[]{:S(2)}) copy-start(s32[64,8]{0,1:T(8,128)} %param.11) | copy-start | bytes 6148
  3.3 1.4 %collective-permute-start = (bf16[13,32,128]{2,1,0:T(8,128)(2,1)S(1)}, bf16[13,32,128]{2,1,0:T(8,128)(2,1)S(1)}, u32[]{:S(2)}, u32[]{:S(2)}) collective-permute-start(bf16[13,32,128]{2,1,0:T(8,128)(2,1)S(1)} %get-tuple-element.15), channel_id=1, source_target_pairs={{0,1},{1,0},{4,5},{5,4},{8,9},{9,8},{12,13},{13,12},{2,3},{3,2},{6... | collective-permute-start | bytes 319496 | tf_op jit(solution)/shard_map/ppermute | solution.py:271
  4.7 3.6 %collective-permute-start.1 = (bf16[2,32,128]{2,1,0:T(8,128)(2,1)S(1)}, bf16[2,32,128]{2,1,0:T(8,128)(2,1)S(1)}, u32[]{:S(2)}, u32[]{:S(2)}) collective-permute-start(bf16[2,32,128]{2,1,0:T(8,128)(2,1)S(1)} %pad_maximum_fusion.2), channel_id=1, source_target_pairs={{0,4},{1,5},{4,0},{5,1},{8,12},{9,13},{12,8},{13,9},{2,6},{3,7},{6... | collective-permute-start | bytes 49160 | tf_op jit(solution)/shard_map/ppermute | solution.py:278
  8.3 7.6 %collective-permute-start.2 = (bf16[4,32,128]{2,1,0:T(8,128)(2,1)S(1)}, bf16[4,32,128]{2,1,0:T(8,128)(2,1)S(1)}, u32[]{:S(2)}, u32[]{:S(2)}) collective-permute-start(bf16[4,32,128]{2,1,0:T(8,128)(2,1)S(1)} %pad_maximum_fusion.1), channel_id=1, source_target_pairs={{0,8},{1,9},{4,12},{5,13},{8,0},{9,1},{12,4},{13,5},{2,10},{3,11},... | collective-permute-start | bytes 98312 | tf_op jit(solution)/shard_map/ppermute | solution.py:278
  10.7 7.6 %collective-permute-start.3 = (bf16[12,32,128]{2,1,0:T(8,128)(2,1)S(1)}, bf16[12,32,128]{2,1,0:T(8,128)(2,1)S(1)}, u32[]{:S(2)}, u32[]{:S(2)}) collective-permute-start(bf16[12,32,128]{2,1,0:T(8,128)(2,1)S(1)} %get-tuple-element.16), channel_id=1, source_target_pairs={{1,4},{5,8},{9,12},{4,1},{8,5},{12,9},{3,6},{7,10},{11,14},{6,3},{... | collective-permute-start | bytes 294920 | tf_op jit(solution)/shard_map/ppermute | solution.py:273

commit v2 on v1

--- a/solution.py
+++ b/solution.py
@@ -246,7 +246,7 @@
     smem = pl.BlockSpec(memory_space=pltpu.SMEM)
     halo = REACH * leaf // LANES + FREACH * rank // LANES
 
-    parts = 4
+    parts = 2
     pts, bas, tra, coeffs, inner, outer = pl.pallas_call(
         up_kernel,
         out_shape=[
@@ -274,7 +274,7 @@
     roots = jnp.concatenate([inner[halo:], inner_got[halo:]], 0)
     order = [0, 1]
     for step in range(1, rounds):
-        flip = 1 << step
+        flip = size >> step
         got = lax.ppermute(roots, SUBTREE, [(i, i ^ flip) for i in range(size)])
         roots = jnp.concatenate([roots, got], 0)
         order = order + [flip ^ o for o in order]

time: 31.3 us -> 30.2 us (0.965)
  the two profiles are of different devices: /device:TPU:1 before, /device:TPU:9 now
where the time goes in v2:
time: 30.2 us; the launch traced here: 30.1 us
  Pallas kernels  15.9 us (53%)
  starting transfers between devices  9.68 us (32%)
  waiting for transfers between devices  4.39 us (15%)
    pallas_call x1, Pallas kernels, shards(): pl.pallas_call(functools.partial(down_kernel, order), out_shape=jax.Shape...  12.8 us
    ppermute x1, starting transfers between devices, shards(): lax.ppermute(outer, SUBTREE, outer_pairs + [(j, i) for i, j in outer_pairs])  6.5 us
    pallas_call x1, Pallas kernels, shards(): pl.pallas_call(up_kernel, out_shape=[pltpu.VMEM((columns, (boxes + 1) * l...  3.07 us
    ppermute x2, starting transfers between devices, shards(): got = lax.ppermute(roots, SUBTREE, [(i, i ^ flip) for i in range(size)])  2.44 us
    ppermute x1, waiting for transfers between devices, shards(): lax.ppermute(outer, SUBTREE, outer_pairs + [(j, i) for i, j in outer_pairs])  2.26 us
    ppermute x2, waiting for transfers between devices, shards(): got = lax.ppermute(roots, SUBTREE, [(i, i ^ flip) for i in range(size)])  1.18 us
    ppermute x1, waiting for transfers between devices, shards(): inner_got = lax.ppermute(inner, SUBTREE, [(i, i ^ 1) for i in range(size)])  0.95 us
    ppermute x1, starting transfers between devices, shards(): inner_got = lax.ppermute(inner, SUBTREE, [(i, i ^ 1) for i in range(size)])  0.74 us
  transfers between devices with their start and end apart: 4, of which 3 were waited for; matrix products, arithmetic and copies ran while one was open for 0% of the time, Pallas kernels for 0%

profile of v2, /device:TPU:9, one launch (start us, length us, event | category | flops | bytes accessed | tf_op | source)
XLA Modules:
  0.0 30.1 jit_solution(7159007047473069735)
XLA Ops:
  0.0 0.0 copy-start
  0.0 0.0 copy-start.1
  0.0 0.0 copy-start.2
  0.0 0.0 copy-start.3
  0.0 0.0 copy-start.4
  0.0 3.1 %upward.1 = (bf16[32,16640]{1,0:T(8,128)(2,1)S(1)}, bf16[64,64,256]{2,1,0:T(8,128)(2,1)S(1)}, bf16[64,64,64]{2,1,0:T(8,128)(2,1)S(1)}, bf16[65,32,128]{2,1,0:T(8...) custom-call(s32[1]{0:T(128)} %bitcast.place_ref, bf16[32,16384]{1,0:T(8,128)(2,1)} %points.1, ...), custom_call_target="tpu_custom_call" | custom-call | flops 20000000000 | bytes 2097152 | tf_op jit(solution)/shard_map/upward/pallas_call | solution.py:250
  3.1 0.7 %collective-permute-start = (bf16[13,32,128]{2,1,0:T(8,128)(2,1)S(1)}, bf16[13,32,128]{2,1,0:T(8,128)(2,1)S(1)}, u32[]{:S(2)}, u32[]{:S(2)}) collective-permute-start(bf16[13,32,128]{2,1,0:T(8,128)(2,1)S(1)} %get-tuple-element.15), channel_id=1, source_target_pairs={{0,1},{1,0},{4,5},{5,4},{8,9},{9,8},{12,13},{13,12},{2,3},{3,2},{6... | collective-permute-start | bytes 319496 | tf_op jit(solution)/shard_map/ppermute | solution.py:271
  3.9 1.0 %collective-permute-done.refs_8_ = bf16[13,32,128]{2,1,0:T(8,128)(2,1)S(1)} collective-permute-done((bf16[13,32,128]{2,1,0:T(8,128)(2,1)S(1)}, bf16[13,32,128]{2,1,0:T(8,128)(2,1)S(1)}, u32[]{:S(2)}, u32[]{:S(2)}) %collective-permute-start) | collective-permute-done | bytes 106528 | tf_op jit(solution)/shard_map/ppermute | solution.py:271
  4.8 2.3 %collective-permute-start.1 = (bf16[2,32,128]{2,1,0:T(8,128)(2,1)S(1)}, bf16[2,32,128]{2,1,0:T(8,128)(2,1)S(1)}, u32[]{:S(2)}, u32[]{:S(2)}) collective-permute-start(bf16[2,32,128]{2,1,0:T(8,128)(2,1)S(1)} %pad_maximum_fusion.2), channel_id=1, source_target_pairs={{0,8},{1,9},{4,12},{5,13},{8,0},{9,1},{12,4},{13,5},{2,10},{3,11},... | collective-permute-start | bytes 49160 | tf_op jit(solution)/shard_map/ppermute | solution.py:278
  7.1 1.2 %collective-permute-done.1 = bf16[2,32,128]{2,1,0:T(8,128)(2,1)S(1)} collective-permute-done((bf16[2,32,128]{2,1,0:T(8,128)(2,1)S(1)}, bf16[2,32,128]{2,1,0:T(8,128)(2,1)S(1)}, u32[]{:S(2)}, u32[]{:S(2)}) %collective-permute-start.1) | collective-permute-done | bytes 16416 | tf_op jit(solution)/shard_map/ppermute | solution.py:278
  8.3 0.1 collective-permute-start.2
  8.4 6.5 %collective-permute-start.3 = (bf16[12,32,128]{2,1,0:T(8,128)(2,1)S(1)}, bf16[12,32,128]{2,1,0:T(8,128)(2,1)S(1)}, u32[]{:S(2)}, u32[]{:S(2)}) collective-permute-start(bf16[12,32,128]{2,1,0:T(8,128)(2,1)S(1)} %get-tuple-element.16), channel_id=1, source_target_pairs={{1,4},{5,8},{9,12},{4,1},{8,5},{12,9},{3,6},{7,10},{11,14},{6,3},{... | collective-permute-start | bytes 294920 | tf_op jit(solution)/shard_map/ppermute | solution.py:273
  14.9 0.0 collective-permute-done.2
  15.0 2.3 %collective-permute-done.3.refs_9_ = bf16[12,32,128]{2,1,0:T(8,128)(2,1)S(1)} collective-permute-done((bf16[12,32,128]{2,1,0:T(8,128)(2,1)S(1)}, bf16[12,32,128]{2,1,0:T(8,128)(2,1)S(1)}, u32[]{:S(2)}, u32[]{:S(2)}) %collective-permute-start.3) | collective-permute-done | bytes 98336 | tf_op jit(solution)/shard_map/ppermute | solution.py:273
  17.2 0.0 copy-done
  17.2 0.0 copy-done.1
  17.2 0.0 copy-done.2
  17.2 0.0 copy-done.3
  17.2 0.0 copy-done.4
  17.3 12.8 %downward.1 = bf16[32,16384]{1,0:T(8,128)(2,1)} custom-call(s32[1]{0:T(128)} %bitcast.place_ref, s32[5,64]{1,0:T(8,128)S(1)} %bitcast.3, s32[8,64]{1,0:T(8,128)S(1)} %bitcast.4, bf16[32,16640]{1,0:T(8,128)(2,1)S(1)} %get-tuple-element.11.refs_0_, bf16[65,32,128]{2,1,0:T(8,128)(2,1)S(1)} %get-tuple-element.12.refs_1_, ...), custom_call_target="tpu_custom_call" | custom-call | tf_op jit(solution)/shard_map/downward/pallas_call | solution.py:284
  (5 shorter events, 0.0 us)
Async XLA Ops:
  0.0 17.2 %copy-start = (bf16[64,5,256,256]{3,2,1,0:T(8,128)(2,1)S(1)}, bf16[64,5,256,256]{3,2,1,0:T(8,128)(2,1)}, u32[]{:S(2)}) copy-start(bf16[64,5,256,256]{3,2,1,0:T(8,128)(2,1)} %refs_6_.1) | copy-start | bytes 125829120
  0.0 17.2 %copy-start.1 = (bf16[64,64,512]{2,1,0:T(8,128)(2,1)S(1)}, bf16[64,64,512]{2,1,0:T(8,128)(2,1)}, u32[]{:S(2)}) copy-start(bf16[64,64,512]{2,1,0:T(8,128)(2,1)} %refs_4_.1) | copy-start | bytes 12582916
  0.0 17.2 %copy-start.2 = (bf16[1,64,512]{2,1,0:T(8,128)(2,1)S(1)}, bf16[1,64,512]{2,1,0:T(8,128)(2,1)}, u32[]{:S(2)}) copy-start(bf16[1,64,512]{2,1,0:T(8,128)(2,1)} %refs_5_.1) | copy-start | bytes 196612
  0.0 17.2 %copy-start.3 = (s32[64,5]{0,1:T(8,128)S(1)}, s32[64,5]{0,1:T(8,128)}, u32[]{:S(2)}) copy-start(s32[64,5]{0,1:T(8,128)} %param.13) | copy-start | bytes 3844
  0.0 17.2 %copy-start.4 = (s32[64,8]{0,1:T(8,128)S(1)}, s32[64,8]{0,1:T(8,128)}, u32[]{:S(2)}) copy-start(s32[64,8]{0,1:T(8,128)} %param.11) | copy-start | bytes 6148
  3.1 1.7 %collective-permute-start = (bf16[13,32,128]{2,1,0:T(8,128)(2,1)S(1)}, bf16[13,32,128]{2,1,0:T(8,128)(2,1)S(1)}, u32[]{:S(2)}, u32[]{:S(2)}) collective-permute-start(bf16[13,32,128]{2,1,0:T(8,128)(2,1)S(1)} %get-tuple-element.15), channel_id=1, source_target_pairs={{0,1},{1,0},{4,5},{5,4},{8,9},{9,8},{12,13},{13,12},{2,3},{3,2},{6... | collective-permute-start | bytes 319496 | tf_op jit(solution)/shard_map/ppermute | solution.py:271
  4.8 3.5 %collective-permute-start.1 = (bf16[2,32,128]{2,1,0:T(8,128)(2,1)S(1)}, bf16[2,32,128]{2,1,0:T(8,128)(2,1)S(1)}, u32[]{:S(2)}, u32[]{:S(2)}) collective-permute-start(bf16[2,32,128]{2,1,0:T(8,128)(2,1)S(1)} %pad_maximum_fusion.2), channel_id=1, source_target_pairs={{0,8},{1,9},{4,12},{5,13},{8,0},{9,1},{12,4},{13,5},{2,10},{3,11},... | collective-permute-start | bytes 49160 | tf_op jit(solution)/shard_map/ppermute | solution.py:278
  8.3 6.6 %collective-permute-start.2 = (bf16[4,32,128]{2,1,0:T(8,128)(2,1)S(1)}, bf16[4,32,128]{2,1,0:T(8,128)(2,1)S(1)}, u32[]{:S(2)}, u32[]{:S(2)}) collective-permute-start(bf16[4,32,128]{2,1,0:T(8,128)(2,1)S(1)} %pad_maximum_fusion.1), channel_id=1, source_target_pairs={{0,4},{1,5},{4,0},{5,1},{8,12},{9,13},{12,8},{13,9},{2,6},{3,7},{6... | collective-permute-start | bytes 98312 | tf_op jit(solution)/shard_map/ppermute | solution.py:278
  8.4 8.8 %collective-permute-start.3 = (bf16[12,32,128]{2,1,0:T(8,128)(2,1)S(1)}, bf16[12,32,128]{2,1,0:T(8,128)(2,1)S(1)}, u32[]{:S(2)}, u32[]{:S(2)}) collective-permute-start(bf16[12,32,128]{2,1,0:T(8,128)(2,1)S(1)} %get-tuple-element.16), channel_id=1, source_target_pairs={{1,4},{5,8},{9,12},{4,1},{8,5},{12,9},{3,6},{7,10},{11,14},{6,3},{... | collective-permute-start | bytes 294920 | tf_op jit(solution)/shard_map/ppermute | solution.py:273

commit v3 on v2

--- a/solution.py
+++ b/solution.py
@@ -274,6 +274,8 @@
     roots = jnp.concatenate([inner[halo:], inner_got[halo:]], 0)
     order = [0, 1]
     for step in range(1, rounds):
+        if step == rounds - 1:
+            roots, outer_got = lax.optimization_barrier((roots, outer_got))
         flip = size >> step
         got = lax.ppermute(roots, SUBTREE, [(i, i ^ flip) for i in range(size)])
         roots = jnp.concatenate([roots, got], 0)

time: 30.2 us -> 31.3 us (1.036)
  the two profiles are of different devices: /device:TPU:9 before, /device:TPU:0 now
where the time goes in v3:
time: 31.3 us; the launch traced here: 31.2 us
  Pallas kernels  15.9 us (51%)
  starting transfers between devices  11.4 us (36%)
  waiting for transfers between devices  3.77 us (12%)
    pallas_call x1, Pallas kernels, shards(): pl.pallas_call(functools.partial(down_kernel, order), out_shape=jax.Shape...  12.8 us
    ppermute x2, starting transfers between devices, shards(): got = lax.ppermute(roots, SUBTREE, [(i, i ^ flip) for i in range(size)])  10.1 us
    pallas_call x1, Pallas kernels, shards(): pl.pallas_call(up_kernel, out_shape=[pltpu.VMEM((columns, (boxes + 1) * l...  3.07 us
    ppermute x2, waiting for transfers between devices, shards(): got = lax.ppermute(roots, SUBTREE, [(i, i ^ flip) for i in range(size)])  2.81 us
    ppermute x1, waiting for transfers between devices, shards(): inner_got = lax.ppermute(inner, SUBTREE, [(i, i ^ 1) for i in range(size)])  0.95 us
    ppermute x1, starting transfers between devices, shards(): lax.ppermute(outer, SUBTREE, outer_pairs + [(j, i) for i, j in outer_pairs])  0.79 us
  transfers between devices with their start and end apart: 4, of which 3 were waited for; matrix products, arithmetic and copies ran while one was open for 0% of the time, Pallas kernels for 0%

profile of v3, /device:TPU:0, one launch (start us, length us, event | category | flops | bytes accessed | tf_op | source)
XLA Modules:
  0.0 31.2 jit_solution(7404419230533669498)
XLA Ops:
  0.0 0.0 copy-start
  0.0 0.0 copy-start.1
  0.0 0.0 copy-start.2
  0.0 0.0 copy-start.3
  0.0 0.0 copy-start.4
  0.0 3.1 %upward.1 = (bf16[32,16640]{1,0:T(8,128)(2,1)S(1)}, bf16[64,64,256]{2,1,0:T(8,128)(2,1)S(1)}, bf16[64,64,64]{2,1,0:T(8,128)(2,1)S(1)}, bf16[65,32,128]{2,1,0:T(8...) custom-call(s32[1]{0:T(128)} %bitcast.place_ref, bf16[32,16384]{1,0:T(8,128)(2,1)} %points.1, ...), custom_call_target="tpu_custom_call" | custom-call | flops 20000000000 | bytes 2097152 | tf_op jit(solution)/shard_map/upward/pallas_call | solution.py:250
  3.1 0.5 %collective-permute-start = (bf16[13,32,128]{2,1,0:T(8,128)(2,1)S(1)}, bf16[13,32,128]{2,1,0:T(8,128)(2,1)S(1)}, u32[]{:S(2)}, u32[]{:S(2)}) collective-permute-start(bf16[13,32,128]{2,1,0:T(8,128)(2,1)S(1)} %get-tuple-element.17), channel_id=1, source_target_pairs={{0,1},{1,0},{4,5},{5,4},{8,9},{9,8},{12,13},{13,12},{2,3},{3,2},{6... | collective-permute-start | bytes 319496 | tf_op jit(solution)/shard_map/ppermute | solution.py:271
  3.6 1.0 %collective-permute-done.refs_8_ = bf16[13,32,128]{2,1,0:T(8,128)(2,1)S(1)} collective-permute-done((bf16[13,32,128]{2,1,0:T(8,128)(2,1)S(1)}, bf16[13,32,128]{2,1,0:T(8,128)(2,1)S(1)}, u32[]{:S(2)}, u32[]{:S(2)}) %collective-permute-start) | collective-permute-done | bytes 106528 | tf_op jit(solution)/shard_map/ppermute | solution.py:271
  4.6 3.9 %collective-permute-start.1 = (bf16[2,32,128]{2,1,0:T(8,128)(2,1)S(1)}, bf16[2,32,128]{2,1,0:T(8,128)(2,1)S(1)}, u32[]{:S(2)}, u32[]{:S(2)}) collective-permute-start(bf16[2,32,128]{2,1,0:T(8,128)(2,1)S(1)} %pad_maximum_fusion.2), channel_id=1, source_target_pairs={{0,8},{1,9},{4,12},{5,13},{8,0},{9,1},{12,4},{13,5},{2,10},{3,11},... | collective-permute-start | bytes 49160 | tf_op jit(solution)/shard_map/ppermute | solution.py:280
  8.5 0.8 %collective-permute-start.2 = (bf16[12,32,128]{2,1,0:T(8,128)(2,1)S(1)}, bf16[12,32,128]{2,1,0:T(8,128)(2,1)S(1)}, u32[]{:S(2)}, u32[]{:S(2)}) collective-permute-start(bf16[12,32,128]{2,1,0:T(8,128)(2,1)S(1)} %get-tuple-element.18), channel_id=1, source_target_pairs={{1,4},{5,8},{9,12},{4,1},{8,5},{12,9},{3,6},{7,10},{11,14},{6,3},{... | collective-permute-start | bytes 294920 | tf_op jit(solution)/shard_map/ppermute | solution.py:273
  9.3 0.9 %collective-permute-done.1 = bf16[2,32,128]{2,1,0:T(8,128)(2,1)S(1)} collective-permute-done((bf16[2,32,128]{2,1,0:T(8,128)(2,1)S(1)}, bf16[2,32,128]{2,1,0:T(8,128)(2,1)S(1)}, u32[]{:S(2)}, u32[]{:S(2)}) %collective-permute-start.1) | collective-permute-done | bytes 16416 | tf_op jit(solution)/shard_map/ppermute | solution.py:280
  10.3 0.0 collective-permute-done.2.refs_9_
  10.3 6.2 %collective-permute-start.3 = (bf16[4,32,128]{2,1,0:T(8,128)(2,1)S(1)}, bf16[4,32,128]{2,1,0:T(8,128)(2,1)S(1)}, u32[]{:S(2)}, u32[]{:S(2)}) collective-permute-start(bf16[4,32,128]{2,1,0:T(8,128)(2,1)S(1)} %pad_maximum_fusion.1), channel_id=1, source_target_pairs={{0,4},{1,5},{4,0},{5,1},{8,12},{9,13},{12,8},{13,9},{2,6},{3,7},{6... | collective-permute-start | bytes 98312 | tf_op jit(solution)/shard_map/ppermute | solution.py:280
  16.4 1.9 %collective-permute-done.3 = bf16[4,32,128]{2,1,0:T(8,128)(2,1)S(1)} collective-permute-done((bf16[4,32,128]{2,1,0:T(8,128)(2,1)S(1)}, bf16[4,32,128]{2,1,0:T(8,128)(2,1)S(1)}, u32[]{:S(2)}, u32[]{:S(2)}) %collective-permute-start.3) | collective-permute-done | bytes 32800 | tf_op jit(solution)/shard_map/ppermute | solution.py:280
  18.3 0.0 copy-done
  18.3 0.0 copy-done.1
  18.4 0.0 copy-done.2
  18.4 0.0 copy-done.3
  18.4 0.0 copy-done.4
  18.4 12.8 %downward.1 = bf16[32,16384]{1,0:T(8,128)(2,1)} custom-call(s32[1]{0:T(128)} %bitcast.place_ref, s32[5,64]{1,0:T(8,128)S(1)} %bitcast.3, s32[8,64]{1,0:T(8,128)S(1)} %bitcast.4, bf16[32,16640]{1,0:T(8,128)(2,1)S(1)} %get-tuple-element.13.refs_0_, bf16[65,32,128]{2,1,0:T(8,128)(2,1)S(1)} %get-tuple-element.14.refs_1_, ...), custom_call_target="tpu_custom_call" | custom-call | tf_op jit(solution)/shard_map/downward/pallas_call | solution.py:286
  (5 shorter events, 0.0 us)
Async XLA Ops:
  0.0 18.3 %copy-start = (bf16[64,5,256,256]{3,2,1,0:T(8,128)(2,1)S(1)}, bf16[64,5,256,256]{3,2,1,0:T(8,128)(2,1)}, u32[]{:S(2)}) copy-start(bf16[64,5,256,256]{3,2,1,0:T(8,128)(2,1)} %refs_6_.1) | copy-start | bytes 125829120
  0.0 18.3 %copy-start.1 = (bf16[64,64,512]{2,1,0:T(8,128)(2,1)S(1)}, bf16[64,64,512]{2,1,0:T(8,128)(2,1)}, u32[]{:S(2)}) copy-start(bf16[64,64,512]{2,1,0:T(8,128)(2,1)} %refs_4_.1) | copy-start | bytes 12582916
  0.0 18.4 %copy-start.2 = (bf16[1,64,512]{2,1,0:T(8,128)(2,1)S(1)}, bf16[1,64,512]{2,1,0:T(8,128)(2,1)}, u32[]{:S(2)}) copy-start(bf16[1,64,512]{2,1,0:T(8,128)(2,1)} %refs_5_.1) | copy-start | bytes 196612
  0.0 18.4 %copy-start.3 = (s32[64,5]{0,1:T(8,128)S(1)}, s32[64,5]{0,1:T(8,128)}, u32[]{:S(2)}) copy-start(s32[64,5]{0,1:T(8,128)} %param.13) | copy-start | bytes 3844
  0.0 18.4 %copy-start.4 = (s32[64,8]{0,1:T(8,128)S(1)}, s32[64,8]{0,1:T(8,128)}, u32[]{:S(2)}) copy-start(s32[64,8]{0,1:T(8,128)} %param.11) | copy-start | bytes 6148
  3.1 1.5 %collective-permute-start = (bf16[13,32,128]{2,1,0:T(8,128)(2,1)S(1)}, bf16[13,32,128]{2,1,0:T(8,128)(2,1)S(1)}, u32[]{:S(2)}, u32[]{:S(2)}) collective-permute-start(bf16[13,32,128]{2,1,0:T(8,128)(2,1)S(1)} %get-tuple-element.17), channel_id=1, source_target_pairs={{0,1},{1,0},{4,5},{5,4},{8,9},{9,8},{12,13},{13,12},{2,3},{3,2},{6... | collective-permute-start | bytes 319496 | tf_op jit(solution)/shard_map/ppermute | solution.py:271
  4.6 5.7 %collective-permute-start.1 = (bf16[2,32,128]{2,1,0:T(8,128)(2,1)S(1)}, bf16[2,32,128]{2,1,0:T(8,128)(2,1)S(1)}, u32[]{:S(2)}, u32[]{:S(2)}) collective-permute-start(bf16[2,32,128]{2,1,0:T(8,128)(2,1)S(1)} %pad_maximum_fusion.2), channel_id=1, source_target_pairs={{0,8},{1,9},{4,12},{5,13},{8,0},{9,1},{12,4},{13,5},{2,10},{3,11},... | collective-permute-start | bytes 49160 | tf_op jit(solution)/shard_map/ppermute | solution.py:280
  8.5 1.7 %collective-permute-start.2 = (bf16[12,32,128]{2,1,0:T(8,128)(2,1)S(1)}, bf16[12,32,128]{2,1,0:T(8,128)(2,1)S(1)}, u32[]{:S(2)}, u32[]{:S(2)}) collective-permute-start(bf16[12,32,128]{2,1,0:T(8,128)(2,1)S(1)} %get-tuple-element.18), channel_id=1, source_target_pairs={{1,4},{5,8},{9,12},{4,1},{8,5},{12,9},{3,6},{7,10},{11,14},{6,3},{... | collective-permute-start | bytes 294920 | tf_op jit(solution)/shard_map/ppermute | solution.py:273
  10.3 8.1 %collective-permute-start.3 = (bf16[4,32,128]{2,1,0:T(8,128)(2,1)S(1)}, bf16[4,32,128]{2,1,0:T(8,128)(2,1)S(1)}, u32[]{:S(2)}, u32[]{:S(2)}) collective-permute-start(bf16[4,32,128]{2,1,0:T(8,128)(2,1)S(1)} %pad_maximum_fusion.1), channel_id=1, source_target_pairs={{0,4},{1,5},{4,0},{5,1},{8,12},{9,13},{12,8},{13,9},{2,6},{3,7},{6... | collective-permute-start | bytes 98312 | tf_op jit(solution)/shard_map/ppermute | solution.py:280
